TPU v7x, 512 devices: a whole 4x8x8 slice. The times are simulated.
512 devices in a mesh: code: 128 (over y, z, core), item: 4 (over x).
Axes of the slice: x: 4, y: 8, z: 8, core: 2. Of those that a mesh axis runs over, the one named last changes fastest.
Arguments:
- hidden: bfloat16 [65536, 1024], P(('code', 'item')), may hold values from -80 to 80
- norm_gain: bfloat16 [1024], replicated, may hold values from 0.099609375 to 1.8984375
- first_weight: bfloat16 [1024, 1024], P('item'), may hold values from -0.1875 to 0.1875
- second_weight: bfloat16 [1024, 1024], P('item'), may hold values from -0.1875 to 0.1875
- codes: int32 [65536, 3], P(('code', 'item')), may hold values from 0 to 8191, as said below
- codebook: float32 [3, 8192, 1024], P(None, 'code'), may hold values from -3 to 3
- embed_avg: float32 [3, 8192, 1024], P(None, 'code'), may hold values from -24 to 24
- cluster_size: float32 [3, 8192], P(None, 'code'), may hold values from 4 to 64
Outputs:
- residual: bfloat16 [65536, 1024], P(('code', 'item'))
- cluster_new: float32 [3, 8192], P(None, 'code')
- avg_new: float32 [3, 8192, 1024], P(None, 'code')
- codebook_new: float32 [3, 8192, 1024], P(None, 'code')
Inputs may be any that keep to these rules, and one draw needn't show every extreme that they name: `codes`: among the items of one device (aligned blocks of 128 rows), at most 2 have, at one level, a code whose value divided by 64 is the same; at every level of every block some such quotient is shared by exactly 2 items.
All inputs are finite; a program needn't handle non-finite values.
Results may differ from a plain program's by a relative error of at most 0.0053.
Values may be sent and summed in bfloat16 or wider, within the bound.
A program may use at most 64 MiB of HBM per device.

v0:
```python
import jax
import jax.numpy as jnp
from jax import lax
from jax.sharding import PartitionSpec as P

ema_decay = 0.8
norm_eps = 1e-06


def rms_scaled(hidden, norm_gain):
    values = hidden.astype(jnp.float32)
    power = jnp.mean(values * values, axis=-1, keepdims=True)
    return (values * lax.rsqrt(power + norm_eps) * norm_gain.astype(jnp.float32)).astype(
        jnp.bfloat16
    )


def route(code_column, code_dev, owners, capacity):
    owner = code_column // code_dev
    local = code_column % code_dev
    match = (owner[:, None] == jnp.arange(owners, dtype=jnp.int32)[None, :]).astype(jnp.int32)
    before = jnp.cumsum(match, axis=0) - match
    rank = jnp.sum(before * match, axis=1)
    return (owner * capacity + rank, local)


def owner_stats(got_rows, got_index, code_dev):
    member = got_index[:, None] == jnp.arange(code_dev, dtype=jnp.int32)[None, :]
    onehot = member.astype(jnp.bfloat16)
    sums = lax.dot_general(
        onehot, got_rows, (((0,), (0,)), ((), ())), preferred_element_type=jnp.float32
    )
    counts = jnp.sum(member.astype(jnp.float32), axis=0)
    return (counts, sums)


def lookup(book_level, got_index):
    picked = jnp.take(book_level, jnp.maximum(got_index, 0), axis=0)
    return jnp.where((got_index >= 0)[:, None], picked, 0.0).astype(jnp.bfloat16)


def place_rows(values, slot, slots):
    return jnp.zeros((slots, values.shape[1]), values.dtype).at[slot].set(values)


def place_index(local, slot, slots):
    return jnp.full((slots,), -1, jnp.int32).at[slot].set(local)


def body(hidden, norm_gain, first_weight, second_weight, codes, codebook, embed_avg, cluster_size):
    rows, width = hidden.shape
    owners = lax.axis_size("code")
    levels = codebook.shape[0]
    code_dev = codebook.shape[1]
    capacity = max(2, 3 * rows // (2 * owners))
    slots = owners * capacity
    normed = rms_scaled(hidden, norm_gain)
    columns = normed
    pre = jnp.dot(
        columns,
        lax.all_gather(first_weight, "item", axis=0, tiled=True),
        preferred_element_type=jnp.float32,
    )
    middle = jax.nn.silu(pre).astype(jnp.bfloat16)
    columns = middle
    resid = jnp.dot(
        columns,
        lax.all_gather(second_weight, "item", axis=0, tiled=True),
        preferred_element_type=jnp.float32,
    )
    placed = [route(codes[:, level], code_dev, owners, capacity) for level in range(levels)]
    count_list = []
    sum_list = []
    for level in range(levels):
        slot, local = placed[level]
        sent = place_rows(resid.astype(jnp.bfloat16), slot, slots)
        index = place_index(local, slot, slots)
        got_rows, got_index = (
            lax.all_to_all(sent, "code", split_axis=0, concat_axis=0, tiled=True),
            lax.all_to_all(index, "code", split_axis=0, concat_axis=0, tiled=True),
        )
        counts, sums = owner_stats(got_rows, got_index, code_dev)
        count_list.append(counts)
        sum_list.append(sums)
        reply = lookup(codebook[level], got_index)
        back = lax.all_to_all(reply, "code", split_axis=0, concat_axis=0, tiled=True)
        resid = resid - back[slot].astype(jnp.float32)
    counts = jnp.stack(count_list)
    sums = jnp.stack(sum_list)
    counts, sums = (
        lax.psum(counts.astype(jnp.bfloat16), "item").astype(jnp.float32),
        lax.psum(sums.astype(jnp.bfloat16), "item").astype(jnp.float32),
    )
    cluster_new = ema_decay * cluster_size + (1.0 - ema_decay) * counts
    avg_new = ema_decay * embed_avg + (1.0 - ema_decay) * sums
    codebook_new = avg_new / cluster_new[:, :, None]
    return (resid.astype(jnp.bfloat16), cluster_new, avg_new, codebook_new)


def solution(mesh):
    in_specs = (
        P(("code", "item"), None),
        P(),
        P("item", None),
        P("item", None),
        P(("code", "item"), None),
        P(None, "code", None),
        P(None, "code", None),
        P(None, "code"),
    )
    out_specs = (
        P(("code", "item"), None),
        P(None, "code"),
        P(None, "code", None),
        P(None, "code", None),
    )
    return jax.shard_map(body, mesh=mesh, in_specs=in_specs, out_specs=out_specs, check_vma=False)
```

profile of v0, /device:TPU:8, one launch (start us, length us, event | category | flops | bytes accessed | tf_op | source)
XLA Modules:
  0.0 301.3 jit_solution(850350447491599808)
XLA Ops:
  11.7 17.4 %all-to-all-start = ((s32[128,2,1]{1,2,0:T(1,128)}), s32[128,2,1]{1,2,0:T(1,128)S(1)}, u32[]{:S(2)}, u32[]{:S(2)}) async-start(s32[128,2,1]{1,2,0:T(1,128)} %bitcast.4), calls=%async_computation | async-start | bytes 131072 | tf_op jit(solution)/shard_map/all_to_all | solution.py:80
  29.9 1.2 slice_bitcast_fusion.2
  35.5 4.4 %all-to-all-done = s32[128,2,1]{1,2,0:T(1,128)S(1)} async-done(((s32[128,2,1]{1,2,0:T(1,128)}), s32[128,2,1]{1,2,0:T(1,128)S(1)}, u32[]{:S(2)}, u32[]{:S(2)}) %all-to-all-start) | async-done | bytes 1056 | tf_op jit(solution)/shard_map/all_to_all | solution.py:80
  39.9 9.3 %all-to-all-start.2 = ((s32[128,2,1]{1,2,0:T(1,128)}), s32[128,2,1]{1,2,0:T(1,128)S(1)}, u32[]{:S(2)}, u32[]{:S(2)}) async-start(s32[128,2,1]{1,2,0:T(1,128)} %bitcast.10), calls=%async_computation.2 | async-start | bytes 131072 | tf_op jit(solution)/shard_map/all_to_all | solution.py:80
  50.7 1.2 gather_fusion.3
  51.9 8.1 %all-to-all-done.2 = s32[128,2,1]{1,2,0:T(1,128)S(1)} async-done(((s32[128,2,1]{1,2,0:T(1,128)}), s32[128,2,1]{1,2,0:T(1,128)S(1)}, u32[]{:S(2)}, u32[]{:S(2)}) %all-to-all-start.2) | async-done | bytes 1056 | tf_op jit(solution)/shard_map/all_to_all | solution.py:80
  60.0 6.5 %all-to-all-start.4 = ((s32[128,2,1]{1,2,0:T(1,128)}), s32[128,2,1]{1,2,0:T(1,128)S(1)}, u32[]{:S(2)}, u32[]{:S(2)}) async-start(s32[128,2,1]{1,2,0:T(1,128)} %bitcast.16), calls=%async_computation.4 | async-start | bytes 131072 | tf_op jit(solution)/shard_map/all_to_all | solution.py:80
  66.7 1.0 all_to_all.75
  67.7 9.6 %all-to-all-done.4 = s32[128,2,1]{1,2,0:T(1,128)S(1)} async-done(((s32[128,2,1]{1,2,0:T(1,128)}), s32[128,2,1]{1,2,0:T(1,128)S(1)}, u32[]{:S(2)}, u32[]{:S(2)}) %all-to-all-start.4) | async-done | bytes 1056 | tf_op jit(solution)/shard_map/all_to_all | solution.py:80
  77.3 6.5 %all-to-all-start.1 = ((bf16[128,2,1024]{2,1,0:T(2,128)(2,1)}), bf16[128,2,1024]{2,1,0:T(2,128)(2,1)S(1)}, u32[]{:S(2)}, u32[]{:S(2)}) async-start(bf16[128,2,1024]{2,1,0:T(2,128)(2,1)} %all_to_all.75), calls=%async_computation.1 | async-start | bytes 1048576 | tf_op jit(solution)/shard_map/all_to_all | solution.py:86
  84.8 1.2 gather_fusion.4
  86.2 1.0 all_to_all.81
  87.2 16.9 %all-to-all-done.1 = bf16[128,2,1024]{2,1,0:T(2,128)(2,1)S(1)} async-done(((bf16[128,2,1024]{2,1,0:T(2,128)(2,1)}), bf16[128,2,1024]{2,1,0:T(2,128)(2,1)S(1)}, u32[]{:S(2)}, u32[]{:S(2)}) %all-to-all-start.1) | async-done | bytes 524320 | tf_op jit(solution)/shard_map/all_to_all | solution.py:86
  104.1 6.4 %all-to-all-start.3 = ((bf16[128,2,1024]{2,1,0:T(2,128)(2,1)}), bf16[128,2,1024]{2,1,0:T(2,128)(2,1)S(1)}, u32[]{:S(2)}, u32[]{:S(2)}) async-start(bf16[128,2,1024]{2,1,0:T(2,128)(2,1)} %all_to_all.81), calls=%async_computation.3 | async-start | bytes 1048576 | tf_op jit(solution)/shard_map/all_to_all | solution.py:86
  111.5 1.2 gather_fusion.5
  113.0 1.0 all_to_all.87
  113.9 16.9 %all-to-all-done.3 = bf16[128,2,1024]{2,1,0:T(2,128)(2,1)S(1)} async-done(((bf16[128,2,1024]{2,1,0:T(2,128)(2,1)}), bf16[128,2,1024]{2,1,0:T(2,128)(2,1)S(1)}, u32[]{:S(2)}, u32[]{:S(2)}) %all-to-all-start.3) | async-done | bytes 524320 | tf_op jit(solution)/shard_map/all_to_all | solution.py:86
  130.8 6.4 %all-to-all-start.5 = ((bf16[128,2,1024]{2,1,0:T(2,128)(2,1)}), bf16[128,2,1024]{2,1,0:T(2,128)(2,1)S(1)}, u32[]{:S(2)}, u32[]{:S(2)}) async-start(bf16[128,2,1024]{2,1,0:T(2,128)(2,1)} %all_to_all.87), calls=%async_computation.5 | async-start | bytes 1048576 | tf_op jit(solution)/shard_map/all_to_all | solution.py:86
  139.6 18.0 %all-to-all-done.5 = bf16[128,2,1024]{2,1,0:T(2,128)(2,1)S(1)} async-done(((bf16[128,2,1024]{2,1,0:T(2,128)(2,1)}), bf16[128,2,1024]{2,1,0:T(2,128)(2,1)S(1)}, u32[]{:S(2)}, u32[]{:S(2)}) %all-to-all-start.5) | async-done | bytes 524320 | tf_op jit(solution)/shard_map/all_to_all | solution.py:86
  158.7 3.9 %subtract_convert_fusion = (bf16[128,1024]{1,0:T(8,128)(2,1)}, f32[128,1024]{1,0:T(8,128)S(1)}) fusion(bf16[128,1024]{1,0:T(8,128)(2,1)S(1)} %gather_fusion.2, bf16[128,1024]{1,0:T(8,128)(2,1)S(1)} %gather_fusion.1, bf16[128,1024]{1,0:T(8,128)(2,1)S(1)} %gather_fusion, bf16[1024,1024]{1,0:T(8,128)(2,1)} %all-gather.5.cloned.1.call-done, ...), kind=kOutput, calls=%fused_computation.30 | convolution fusion | flops 538968064 | bytes 6033920 | tf_op jit(solution)/shard_map/dot_general | solution.py:66
  162.5 1.3 scatter_custom_fusion.4
  164.9 6.6 %all-to-all-start.7 = ((bf16[128,2,1024]{2,1,0:T(2,128)(2,1)}), bf16[128,2,1024]{2,1,0:T(2,128)(2,1)S(1)}, u32[]{:S(2)}, u32[]{:S(2)}) async-start(bf16[128,2,1024]{2,1,0:T(2,128)(2,1)} %all_to_all.93), calls=%async_computation.7 | async-start | bytes 1048576 | tf_op jit(solution)/shard_map/all_to_all | solution.py:79
  171.5 1.3 scatter_custom_fusion.3
  173.8 18.0 %all-to-all-done.7 = bf16[128,2,1024]{2,1,0:T(2,128)(2,1)S(1)} async-done(((bf16[128,2,1024]{2,1,0:T(2,128)(2,1)}), bf16[128,2,1024]{2,1,0:T(2,128)(2,1)S(1)}, u32[]{:S(2)}, u32[]{:S(2)}) %all-to-all-start.7) | async-done | bytes 524320 | tf_op jit(solution)/shard_map/all_to_all | solution.py:79
  191.8 6.4 %all-to-all-start.6 = ((bf16[128,2,1024]{2,1,0:T(2,128)(2,1)}), bf16[128,2,1024]{2,1,0:T(2,128)(2,1)S(1)}, u32[]{:S(2)}, u32[]{:S(2)}) async-start(bf16[128,2,1024]{2,1,0:T(2,128)(2,1)} %all_to_all.90), calls=%async_computation.6 | async-start | bytes 1048576 | tf_op jit(solution)/shard_map/all_to_all | solution.py:79
  198.2 1.3 scatter_custom_fusion.5
  200.5 18.0 %all-to-all-done.6 = bf16[128,2,1024]{2,1,0:T(2,128)(2,1)S(1)} async-done(((bf16[128,2,1024]{2,1,0:T(2,128)(2,1)}), bf16[128,2,1024]{2,1,0:T(2,128)(2,1)S(1)}, u32[]{:S(2)}, u32[]{:S(2)}) %all-to-all-start.6) | async-done | bytes 524320 | tf_op jit(solution)/shard_map/all_to_all | solution.py:79
  218.5 6.4 %all-to-all-start.8 = ((bf16[128,2,1024]{2,1,0:T(2,128)(2,1)}), bf16[128,2,1024]{2,1,0:T(2,128)(2,1)S(1)}, u32[]{:S(2)}, u32[]{:S(2)}) async-start(bf16[128,2,1024]{2,1,0:T(2,128)(2,1)} %all_to_all.96), calls=%async_computation.8 | async-start | bytes 1048576 | tf_op jit(solution)/shard_map/all_to_all | solution.py:79
  226.0 19.2 %all-to-all-done.8 = bf16[128,2,1024]{2,1,0:T(2,128)(2,1)S(1)} async-done(((bf16[128,2,1024]{2,1,0:T(2,128)(2,1)}), bf16[128,2,1024]{2,1,0:T(2,128)(2,1)S(1)}, u32[]{:S(2)}, u32[]{:S(2)}) %all-to-all-start.8) | async-done | bytes 524320 | tf_op jit(solution)/shard_map/all_to_all | solution.py:79
  246.6 10.5 %psum.14 = bf16[3,64]{1,0:T(4,128)(2,1)S(1)} all-reduce(bf16[3,64]{1,0:T(4,128)(2,1)S(1)} %pad_maximum_fusion.1), channel_id=1, replica_groups=mesh['code'=128,'item'=4] {'item'}, use_global_device_ids=true, to_apply=%region_13.15 | all-reduce | flops 192 | bytes 768 | tf_op jit(solution)/shard_map/psum | solution.py:91
  257.1 35.3 %all-reduce.2.cloned.1.call-done = bf16[3,64,1024]{2,1,0:T(8,128)(2,1)} async-done(((bf16[3,64,1024]{2,1,0:T(8,128)(2,1)}), bf16[3,64,1024]{2,1,0:T(8,128)(2,1)}) %all-reduce.2.cloned.1.call-update) | async-done | bytes 393232 | tf_op jit(solution)/shard_map/psum | solution.py:92
  292.4 2.3 broadcast_divide_fusion
  (84 shorter events, 22.5 us)
Async XLA Ops:
  7.2 151.5 %all-gather.3.cloned.1.call-start = ((), (), s32[]{:S(2)}) async-start(), calls=%async_computation.9 | async-start | bytes 2621440 | tf_op jit(solution)/shard_map/all_gather | solution.py:61
  11.7 28.2 %all-to-all-start = ((s32[128,2,1]{1,2,0:T(1,128)}), s32[128,2,1]{1,2,0:T(1,128)S(1)}, u32[]{:S(2)}, u32[]{:S(2)}) async-start(s32[128,2,1]{1,2,0:T(1,128)} %bitcast.4), calls=%async_computation | async-start | bytes 131072 | tf_op jit(solution)/shard_map/all_to_all | solution.py:80
  29.1 129.6 %all-gather.5.cloned.1.call-start = ((), (), s32[]{:S(2)}) async-start(), calls=%async_computation.10 | async-start | bytes 2621440 | tf_op jit(solution)/shard_map/all_gather | solution.py:68
  39.9 20.1 %all-to-all-start.2 = ((s32[128,2,1]{1,2,0:T(1,128)}), s32[128,2,1]{1,2,0:T(1,128)S(1)}, u32[]{:S(2)}, u32[]{:S(2)}) async-start(s32[128,2,1]{1,2,0:T(1,128)} %bitcast.10), calls=%async_computation.2 | async-start | bytes 131072 | tf_op jit(solution)/shard_map/all_to_all | solution.py:80
  60.0 17.3 %all-to-all-start.4 = ((s32[128,2,1]{1,2,0:T(1,128)}), s32[128,2,1]{1,2,0:T(1,128)S(1)}, u32[]{:S(2)}, u32[]{:S(2)}) async-start(s32[128,2,1]{1,2,0:T(1,128)} %bitcast.16), calls=%async_computation.4 | async-start | bytes 131072 | tf_op jit(solution)/shard_map/all_to_all | solution.py:80
  77.3 26.9 %all-to-all-start.1 = ((bf16[128,2,1024]{2,1,0:T(2,128)(2,1)}), bf16[128,2,1024]{2,1,0:T(2,128)(2,1)S(1)}, u32[]{:S(2)}, u32[]{:S(2)}) async-start(bf16[128,2,1024]{2,1,0:T(2,128)(2,1)} %all_to_all.75), calls=%async_computation.1 | async-start | bytes 1048576 | tf_op jit(solution)/shard_map/all_to_all | solution.py:86
  104.1 26.7 %all-to-all-start.3 = ((bf16[128,2,1024]{2,1,0:T(2,128)(2,1)}), bf16[128,2,1024]{2,1,0:T(2,128)(2,1)S(1)}, u32[]{:S(2)}, u32[]{:S(2)}) async-start(bf16[128,2,1024]{2,1,0:T(2,128)(2,1)} %all_to_all.81), calls=%async_computation.3 | async-start | bytes 1048576 | tf_op jit(solution)/shard_map/all_to_all | solution.py:86
  112.7 24.6 %copy-start.3 = (bf16[1024]{0:T(1024)(128)(2,1)S(1)}, bf16[1024]{0:T(1024)(128)(2,1)}, u32[]{:S(2)}) copy-start(bf16[1024]{0:T(1024)(128)(2,1)} %param.11) | copy-start | bytes 6148
  112.7 24.6 %copy-start.1 = (bf16[128,1024]{1,0:T(8,128)(2,1)S(1)}, bf16[128,1024]{1,0:T(8,128)(2,1)}, u32[]{:S(2)}) copy-start(bf16[128,1024]{1,0:T(8,128)(2,1)} %param.10) | copy-start | bytes 786436
  130.8 26.7 %all-to-all-start.5 = ((bf16[128,2,1024]{2,1,0:T(2,128)(2,1)}), bf16[128,2,1024]{2,1,0:T(2,128)(2,1)S(1)}, u32[]{:S(2)}, u32[]{:S(2)}) async-start(bf16[128,2,1024]{2,1,0:T(2,128)(2,1)} %all_to_all.87), calls=%async_computation.5 | async-start | bytes 1048576 | tf_op jit(solution)/shard_map/all_to_all | solution.py:86
  164.9 26.9 %all-to-all-start.7 = ((bf16[128,2,1024]{2,1,0:T(2,128)(2,1)}), bf16[128,2,1024]{2,1,0:T(2,128)(2,1)S(1)}, u32[]{:S(2)}, u32[]{:S(2)}) async-start(bf16[128,2,1024]{2,1,0:T(2,128)(2,1)} %all_to_all.93), calls=%async_computation.7 | async-start | bytes 1048576 | tf_op jit(solution)/shard_map/all_to_all | solution.py:79
  191.8 26.7 %all-to-all-start.6 = ((bf16[128,2,1024]{2,1,0:T(2,128)(2,1)}), bf16[128,2,1024]{2,1,0:T(2,128)(2,1)S(1)}, u32[]{:S(2)}, u32[]{:S(2)}) async-start(bf16[128,2,1024]{2,1,0:T(2,128)(2,1)} %all_to_all.90), calls=%async_computation.6 | async-start | bytes 1048576 | tf_op jit(solution)/shard_map/all_to_all | solution.py:79
  218.5 26.7 %all-to-all-start.8 = ((bf16[128,2,1024]{2,1,0:T(2,128)(2,1)}), bf16[128,2,1024]{2,1,0:T(2,128)(2,1)S(1)}, u32[]{:S(2)}, u32[]{:S(2)}) async-start(bf16[128,2,1024]{2,1,0:T(2,128)(2,1)} %all_to_all.96), calls=%async_computation.8 | async-start | bytes 1048576 | tf_op jit(solution)/shard_map/all_to_all | solution.py:79
  224.9 67.5 %all-reduce.2.cloned.1.call-start = ((), (), s32[]{:S(2)}) async-start(), calls=%async_computation.11 | async-start | bytes 786432 | tf_op jit(solution)/shard_map/psum | solution.py:92
  225.6 31.5 %copy-start.4 = (f32[3,64]{1,0:T(4,128)S(1)}, f32[3,64]{1,0:T(4,128)}, u32[]{:S(2)}) copy-start(f32[3,64]{1,0:T(4,128)} %param.17) | copy-start | bytes 2308
  225.6 66.8 %copy-start = (f32[3,64,1024]{2,1,0:T(8,128)S(1)}, f32[3,64,1024]{2,1,0:T(8,128)}, u32[]{:S(2)}) copy-start(f32[3,64,1024]{2,1,0:T(8,128)} %param.16) | copy-start | bytes 2359300
  257.1 37.7 %copy-start.2 = (f32[3,64]{1,0:T(4,128)}, f32[3,64]{1,0:T(4,128)S(1)}, u32[]{:S(2)}) copy-start(f32[3,64]{1,0:T(4,128)S(1)} %multiply_add_fusion.1) | copy-start | bytes 2308
Sparse Core Ops, SparseCore 0:
  10.1 40.7 all-gather.2
  53.0 36.2 all-gather.4
  246.6 45.8 all-reduce.1
where the time goes:
time: 302 us; the launch traced here: 301 us
  waiting for transfers between devices  166 us (55%)
  starting transfers between devices  72 us (24%)
  local copies, waits for them, and re-layouts  20.6 us (7%)
  between operations  14.2 us (5%)
  other arithmetic  13.7 us (5%)
  blocking collectives  10.5 us (3%)
  matrix products  4.5 us (1%)
    all_to_all x3, waiting for transfers between devices, body(): lax.all_to_all(sent, 'code', split_axis=0, concat_axis=0, tiled=True)  55.2 us
    all_to_all x3, waiting for transfers between devices, body(): lax.all_to_all(reply, 'code', split_axis=0, concat_axis=0, tiled=True)  51.8 us
    psum x1, waiting for transfers between devices, body(): lax.psum(sums.astype(jnp.bfloat16), 'item').astype(jnp.float32)  35.3 us
    all_to_all x3, starting transfers between devices, body(): lax.all_to_all(index, 'code', split_axis=0, concat_axis=0, tiled=True)  33.2 us
    all_to_all x3, waiting for transfers between devices, body(): lax.all_to_all(index, 'code', split_axis=0, concat_axis=0, tiled=True)  22.1 us
    all_to_all x3, starting transfers between devices, body(): lax.all_to_all(sent, 'code', split_axis=0, concat_axis=0, tiled=True)  19.4 us
    all_to_all x3, starting transfers between devices, body(): lax.all_to_all(reply, 'code', split_axis=0, concat_axis=0, tiled=True)  19.3 us
    psum x1, blocking collectives, body(): lax.psum(counts.astype(jnp.bfloat16), 'item').astype(jnp.float32)  10.5 us
  transfers between devices with their start and end apart: 12, of which 10 were waited for; matrix products, arithmetic and copies ran while one was open for 7% of the time, Pallas kernels for 0%

commit v1 on v0

v1 whole, which is shorter than its diff:
```python
import functools

import jax
import jax.numpy as jnp
from jax import lax
from jax.experimental import pallas as pl
from jax.experimental.pallas import tpu as pltpu
from jax.sharding import PartitionSpec as P

ema_decay = 0.8
norm_eps = 1e-06
MESH = pl.DeviceIdType.MESH
LANES = 128
CHUNKS = 8
CORES = 2
F32, BF16, I32 = jnp.float32, jnp.bfloat16, jnp.int32


def grid_of(owners):
    side = 8 if owners == 128 else 2
    return side, side


def iota(shape, axis):
    return lax.broadcasted_iota(I32, shape, axis)


def kernel(
    cfg,
    hidden_ref, gain_ref, w1_ref, w2_ref, codes_ref, codes_t_ref, book_ref, embed_ref, size_ref,
    resid_out, cluster_out, avg_out, new_out,
    hid, book, embed, w1, w2, outv, avgv, newv,
    flat8, book8, r8, tot8, onehot, idxexp,
    table, items, slots, zgot, ysrc, ygot, want, picked, xcount,
    items_s, slots_s, want_s,
    qsend0, qsend1, qsend2, qrecv0, qrecv1, qrecv2,
    rsend0, rsend1, rsend2, rrecv0, rrecv1, rrecv2,
    xsum0, xsum1, xsum2,
    lsem, ssem, zsend, zrecv, ysend, yrecv, wsend, wrecv, fsend, frecv,
    qss, qrs, rss, rrs, xss, xrs, css, crs, osem,
):
    ny, nz, nx, rows, levels, code_dev = cfg
    owners = ny * nz * CORES
    nyc = ny * CORES
    width = nz * 16
    qsend, qrecv = (qsend0, qsend1, qsend2), (qrecv0, qrecv1, qrecv2)
    rsend, rrecv = (rsend0, rsend1, rsend2), (rrecv0, rrecv1, rrecv2)
    xsum = (xsum0, xsum1, xsum2)
    me = lax.axis_index("code")
    xi = lax.axis_index("item")
    core = me % CORES
    z = (me // CORES) % nz
    y = me // (CORES * nz)
    yc = y * CORES + core
    sibling = me + 1 - 2 * core

    def code_id(ty, tz, tc):
        return (ty * nz + tz) * CORES + tc

    def zmate(k):
        tz = (z + k) % nz
        return tz, code_id(y, tz, core)

    def ymate(k):
        tc = (core + k) % CORES
        ty = (y + k // CORES) % ny
        return ty, tc, code_id(ty, z, tc)

    def partner(k):
        d = k // CORES
        dz = d % nz
        tc = (core + k) % CORES
        tz = (z + dz) % nz
        ty = (y + dz + d // nz) % ny
        return code_id(ty, tz, tc), (ty * CORES + tc), tz

    def loop(low, high, step, unroll=1):
        def go(k, _):
            step(k)
            return 0

        lax.fori_loop(low, high, go, 0, unroll=unroll)

    def wait_bytes(view, sem):
        pltpu.make_async_copy(view, view, sem).wait()

    loads = [
        pltpu.make_async_copy(hidden_ref, hid, lsem.at[0]),
        pltpu.make_async_copy(book_ref, book, lsem.at[1]),
        pltpu.make_async_copy(w1_ref, w1.at[xi], lsem.at[2]),
        pltpu.make_async_copy(w2_ref, w2.at[xi], lsem.at[3]),
        pltpu.make_async_copy(embed_ref, embed, lsem.at[4]),
    ]
    for one in loads:
        one.start()

    barrier = pltpu.get_barrier_semaphore()

    def greet(device):
        pl.semaphore_signal(barrier, inc=1, device_id=device, device_id_type=MESH)

    loop(1, nz, lambda k: greet({"code": zmate(k)[1]}))
    loop(1, nyc, lambda k: greet({"code": ymate(k)[2]}))
    for d in range(1, nx):
        greet({"item": (xi + d) % nx})

    lane = iota((rows, LANES), 1)
    down, across = iota((rows, rows), 0), iota((rows, rows), 1)
    to_lane = iota((owners, LANES), 1)
    to_sub = iota((owners, rows), 0)
    requests = jnp.zeros((owners, LANES), I32)
    items[...] = jnp.zeros(items.shape, I32)
    slots[...] = jnp.zeros(slots.shape, I32)
    for level in range(levels):
        code_col, code_row = codes_ref[:, level : level + 1], codes_t_ref[level : level + 1, :]
        owner_col, owner_row = code_col // code_dev, code_row // code_dev
        same = owner_col == owner_row
        rank_row = jnp.sum(jnp.where(same & (down < across), 1, 0), axis=0, keepdims=True)
        rank_col = jnp.sum(jnp.where(same & (across < down), 1, 0), axis=1, keepdims=True)
        slots[level : level + 1, :rows] = owner_row
        slots[levels + level : levels + level + 1, :rows] = rank_row
        ring = owner_row // CORES % nz * nyc + owner_row // (CORES * nz) * CORES + owner_row % CORES
        for k in range(2):
            at = 2 * level + k
            chosen = jnp.where((to_sub == ring) & (rank_row == k), code_row % code_dev + 1, 0)
            local = jnp.sum(chosen, axis=1, keepdims=True)
            requests = jnp.where(to_lane == z * 8 + at, local, requests)
            number = jnp.where((lane == owner_col) & (rank_col == k), iota((rows, LANES), 0), 0)
            items[at : at + 1, :] = jnp.sum(number, axis=0, keepdims=True)
    table[...] = requests
    to_smem = [
        pltpu.make_async_copy(items, items_s, ssem.at[0]),
        pltpu.make_async_copy(slots, slots_s, ssem.at[1]),
    ]
    for one in to_smem:
        one.start()

    loads[0].wait()
    values = hid[...].astype(F32)
    power = jnp.mean(values * values, axis=-1, keepdims=True)
    normed = (values * lax.rsqrt(power + norm_eps) * gain_ref[...].astype(F32)).astype(BF16)
    hid[...] = normed
    loads[1].wait()
    for level in range(levels):
        for c in range(CHUNKS):
            flat8[pl.ds(c, code_dev, stride=CHUNKS), :] = book[level, :, c * LANES : (c + 1) * LANES]
        book8[level] = flat8[: code_dev * CHUNKS, :].reshape(code_dev, CHUNKS, LANES)
    for one in loads[2:]:
        one.wait()

    pl.semaphore_wait(barrier, nz - 1 + nyc - 1 + nx - 1)

    def ring_rows(tz):
        return pl.ds(pl.multiple_of(tz * nyc, nyc), nyc)

    def send_table(k):
        tz, device = zmate(k)
        pltpu.make_async_remote_copy(
            src_ref=table.at[ring_rows(tz)], dst_ref=zgot.at[z], send_sem=zsend, recv_sem=zrecv,
            device_id={"code": device}, device_id_type=MESH,
        ).start()

    loop(1, nz, send_table)
    zgot[z] = table[ring_rows(z), :]

    half = w1.shape[1] // CORES
    weights = (w1, w2)

    def part(w, source, which):
        return w.at[source, pl.ds(pl.multiple_of(which * half, half), half)]

    def weight_copy(i, d):
        return pltpu.make_async_remote_copy(
            src_ref=part(weights[i], xi, core), dst_ref=part(weights[i], xi, core),
            send_sem=wsend.at[i, d - 1], recv_sem=wrecv.at[i, d - 1],
            device_id={"item": (xi + d) % nx}, device_id_type=MESH,
        )

    def pass_on(i, d):
        source = (xi + nx - d) % nx
        return pltpu.make_async_remote_copy(
            src_ref=part(weights[i], source, core), dst_ref=part(weights[i], source, core),
            send_sem=fsend.at[i, d - 1], recv_sem=frecv.at[i, d - 1],
            device_id={"code": sibling}, device_id_type=MESH,
        )

    for i in range(2):
        for d in range(1, nx):
            weight_copy(i, d).start()

    wait_bytes(zgot.at[pl.ds(0, nz - 1)], zrecv)
    gathered = zgot[0]
    for s in range(1, nz):
        gathered = gathered + zgot[s]
    ysrc[:nyc, :] = gathered

    def tile_of(at):
        return pl.ds(pl.multiple_of(at // 8 * 8, 8), 8)

    def send_requests(k):
        ty, tc, device = ymate(k)
        pltpu.make_async_remote_copy(
            src_ref=ysrc.at[tile_of(ty * CORES + tc)], dst_ref=ygot.at[yc], send_sem=ysend, recv_sem=yrecv,
            device_id={"code": device}, device_id_type=MESH,
        ).start()

    loop(1, nyc, send_requests)
    ygot[yc] = ysrc[tile_of(yc), :]
    for one in to_smem:
        one.wait()
    wait_bytes(ygot.at[pl.ds(0, nyc - 1)], yrecv)
    mine = iota((nyc, 8, LANES), 1) == yc % 8
    want[...] = jnp.sum(jnp.where(mine, ygot[...], 0), axis=1) - 1
    picked[...] = jnp.maximum(want[...], 0)
    ask = pltpu.make_async_copy(picked, want_s, ssem.at[2])
    ask.start()

    code_row = iota((code_dev, LANES), 0)
    code_lane = iota((code_dev, LANES), 1)
    hist = jnp.zeros((code_dev, LANES), F32)
    for s in range(nyc):
        hist = hist + (want[s : s + 1, :] == code_row).astype(F32)
    xcount[xi] = jnp.zeros((8, LANES), F32)
    for level in range(levels):
        column = jnp.sum(
            jnp.where((code_lane % 8) // 2 == level, hist, 0.0), axis=1, keepdims=True
        )
        xcount[xi, level : level + 1, :] = jnp.sum(
            jnp.where(code_row == code_lane, column, 0.0), axis=0, keepdims=True
        )
    count_copies = [
        pltpu.make_async_remote_copy(
            src_ref=xcount.at[xi], dst_ref=xcount.at[xi], send_sem=css.at[d - 1], recv_sem=crs.at[d - 1],
            device_id={"item": (xi + d) % nx}, device_id_type=MESH,
        )
        for d in range(1, nx)
    ]
    ask.wait()

    def reply(level):
        def block(rs):
            rows_of = [book8[level, want_s[rs[0], rs[1] * 8 + 2 * level + k]] for k in range(2)]
            return jnp.concatenate(rows_of, axis=0).astype(BF16)

        qrecv[level][me] = block((yc, z))

        def one(k):
            device, tyc, tz = partner(k)
            qsend[level][device] = block((tyc, tz))
            pltpu.make_async_remote_copy(
                src_ref=qsend[level].at[device], dst_ref=qrecv[level].at[me],
                send_sem=qss.at[level], recv_sem=qrs.at[level],
                device_id={"code": device}, device_id_type=MESH,
            ).start()

        loop(1, owners, one)

    def send_rows(level):
        def block(owner):
            rows_of = [r8[items_s[2 * level + k, owner]] for k in range(2)]
            return jnp.concatenate(rows_of, axis=0).astype(BF16)

        rrecv[level][yc * nz + z] = block(me)

        def one(k):
            device, _, _ = partner(k)
            rsend[level][device] = block(device)
            pltpu.make_async_remote_copy(
                src_ref=rsend[level].at[device], dst_ref=rrecv[level].at[yc * nz + z],
                send_sem=rss.at[level], recv_sem=rrs.at[level],
                device_id={"code": device}, device_id_type=MESH,
            ).start()

        loop(1, owners, one)

    def subtract(level):
        wait_bytes(qrecv[level].at[pl.ds(0, owners - 1)], qrs.at[level])

        def one(i):
            second = slots_s[levels + level, i].astype(F32)
            pair = qrecv[level][slots_s[level, i]].astype(F32)
            r8[i] = r8[i] - (pair[:CHUNKS] * (1.0 - second) + pair[CHUNKS:] * second)

        loop(0, rows, one, unroll=4)

    reply(0)
    for one in count_copies:
        one.start()
    for d in range(1, nx):
        weight_copy(0, d).wait_recv()
        pass_on(0, d).start()
    reply(1)
    for d in range(1, nx):
        weight_copy(1, d).wait_recv()
        pass_on(1, d).start()

    depth = w1.shape[1] * nx
    for d in range(1, nx):
        pass_on(0, d).wait_recv()
    pre = jnp.dot(hid[...], w1[...].reshape(depth, -1), preferred_element_type=F32)
    middle = (pre / (1.0 + jnp.exp(-pre))).astype(BF16)
    for d in range(1, nx):
        pass_on(1, d).wait_recv()
    first = jnp.dot(middle, w2[...].reshape(depth, -1), preferred_element_type=F32)
    for c in range(CHUNKS):
        flat8[pl.ds(c, rows, stride=CHUNKS), :] = first[:, c * LANES : (c + 1) * LANES]
    r8[...] = flat8[: rows * CHUNKS, :].reshape(rows, CHUNKS, LANES)

    def sum_copy(level, d):
        return pltpu.make_async_remote_copy(
            src_ref=xsum[level].at[xi], dst_ref=xsum[level].at[xi],
            send_sem=xss.at[level, d - 1], recv_sem=xrs.at[level, d - 1],
            device_id={"item": (xi + d) % nx}, device_id_type=MESH,
        )

    def add_up(level):
        spread_from = iota((LANES, width), 0)
        spread_to = iota((LANES, width), 1)
        spread = (spread_from == (spread_to // 16) * 8 + 2 * level + (spread_to % 16) // 8).astype(BF16)
        asked = jnp.dot(want[...].astype(F32).astype(BF16), spread, preferred_element_type=F32)
        idxexp[...] = asked.astype(I32) * CHUNKS + iota((nyc, width), 1) % CHUNKS
        sum_rows = iota((code_dev * CHUNKS, width), 0)
        for s in range(nyc):
            onehot[:, s * width : (s + 1) * width] = (sum_rows == idxexp[s : s + 1, :]).astype(F32).astype(BF16)
        wait_bytes(rrecv[level].at[pl.ds(0, owners - 1)], rrs.at[level])
        got = rrecv[level][...].reshape(owners * 16, LANES)
        sums = jnp.dot(onehot[...], got, preferred_element_type=F32)
        xsum[level][xi] = sums.astype(BF16)
        for d in range(1, nx):
            sum_copy(level, d).start()

    def out_copies(level):
        return (
            pltpu.make_async_copy(avgv.at[level], avg_out.at[level], osem.at[level]),
            pltpu.make_async_copy(newv.at[level], new_out.at[level], osem.at[levels + level]),
        )

    def update(level):
        for d in range(1, nx):
            sum_copy(level, d).wait_recv()
        total = xsum[level][0].astype(F32)
        for x in range(1, nx):
            total = total + xsum[level][x].astype(F32)
        tot8[...] = total
        row = cluster_out[level : level + 1, :]
        same = iota((code_dev, code_dev), 0) == iota((code_dev, code_dev), 1)
        column = jnp.sum(jnp.where(same, row, 0.0), axis=1, keepdims=True)
        for c in range(CHUNKS):
            span = slice(c * LANES, (c + 1) * LANES)
            part_sum = tot8[pl.ds(c, code_dev, stride=CHUNKS), :]
            average = ema_decay * embed[level, :, span] + (1.0 - ema_decay) * part_sum
            avgv[level, :, span] = average
            newv[level, :, span] = average / column
        for one in out_copies(level):
            one.start()

    send_rows(0)
    subtract(0)
    send_rows(1)
    subtract(1)
    send_rows(2)
    for one in count_copies:
        one.wait_recv()
    counts = xcount[0]
    for x in range(1, nx):
        counts = counts + xcount[x]
    cluster_out[...] = ema_decay * size_ref[...] + (1.0 - ema_decay) * counts[:levels, :code_dev]
    add_up(0)
    reply(2)
    add_up(1)
    update(0)
    add_up(2)
    update(1)
    update(2)
    subtract(2)
    flat8[: rows * CHUNKS, :] = r8[...].reshape(rows * CHUNKS, LANES)
    for c in range(CHUNKS):
        outv[:, c * LANES : (c + 1) * LANES] = flat8[pl.ds(c, rows, stride=CHUNKS), :].astype(BF16)
    last = pltpu.make_async_copy(outv, resid_out, osem.at[2 * levels])
    last.start()

    wait_bytes(zgot.at[pl.ds(0, nz - 1)], zsend)
    wait_bytes(ygot.at[pl.ds(0, nyc - 1)], ysend)
    for d in range(1, nx):
        for i in range(2):
            weight_copy(i, d).wait_send()
            pass_on(i, d).wait_send()
        count_copies[d - 1].wait_send()
        for level in range(levels):
            sum_copy(level, d).wait_send()
    for level in range(levels):
        wait_bytes(qrecv[level].at[pl.ds(0, owners - 1)], qss.at[level])
        wait_bytes(rrecv[level].at[pl.ds(0, owners - 1)], rss.at[level])
        for one in out_copies(level):
            one.wait()
    last.wait()


def body(hidden, norm_gain, first_weight, second_weight, codes, codebook, embed_avg, cluster_size):
    rows, width = hidden.shape
    owners = lax.axis_size("code")
    nx = lax.axis_size("item")
    levels, code_dev, _ = codebook.shape
    ny, nz = grid_of(owners)
    nyc = ny * CORES
    cfg = (ny, nz, nx, rows, levels, code_dev)
    vmem, dma = pltpu.VMEM, pltpu.SemaphoreType.DMA
    blocks = [vmem((owners, 16, LANES), BF16)] * 12
    anywhere = pl.BlockSpec(memory_space=pl.ANY)
    inside = pl.BlockSpec(memory_space=pltpu.VMEM)
    shapes = (
        jax.ShapeDtypeStruct((rows, width), BF16),
        jax.ShapeDtypeStruct((levels, code_dev), F32),
        jax.ShapeDtypeStruct((levels, code_dev, width), F32),
        jax.ShapeDtypeStruct((levels, code_dev, width), F32),
    )
    return pl.pallas_call(
        functools.partial(kernel, cfg),
        out_shape=shapes,
        in_specs=[anywhere, inside, anywhere, anywhere, inside, inside, anywhere, anywhere, inside],
        out_specs=(anywhere, inside, anywhere, anywhere),
        scratch_shapes=[
            vmem((rows, width), BF16),
            vmem((levels, code_dev, width), F32),
            vmem((levels, code_dev, width), F32),
            vmem((nx,) + first_weight.shape, BF16),
            vmem((nx,) + second_weight.shape, BF16),
            vmem((rows, width), BF16),
            vmem((levels, code_dev, width), F32),
            vmem((levels, code_dev, width), F32),
            vmem((max(rows, code_dev) * CHUNKS, LANES), F32),
            vmem((levels, code_dev, CHUNKS, LANES), F32),
            vmem((rows, CHUNKS, LANES), F32),
            vmem((code_dev * CHUNKS, LANES), F32),
            vmem((code_dev * CHUNKS, owners * 16), BF16),
            vmem((nyc, nz * 16), I32),
            vmem((owners, LANES), I32),
            vmem((8, LANES), I32),
            vmem((8, LANES), I32),
            vmem((nz, nyc, LANES), I32),
            vmem((max(nyc, 8), LANES), I32),
            vmem((nyc, 8, LANES), I32),
            vmem((nyc, LANES), I32),
            vmem((nyc, LANES), I32),
            vmem((nx, 8, LANES), F32),
            pltpu.SMEM((8, LANES), I32),
            pltpu.SMEM((8, LANES), I32),
            pltpu.SMEM((nyc, LANES), I32),
            *blocks,
            *[vmem((nx, code_dev * CHUNKS, LANES), BF16)] * 3,
            dma((5,)),
            dma((3,)),
            dma,
            dma,
            dma,
            dma,
            dma((2, nx - 1)),
            dma((2, nx - 1)),
            dma((2, nx - 1)),
            dma((2, nx - 1)),
            dma((levels,)),
            dma((levels,)),
            dma((levels,)),
            dma((levels,)),
            dma((levels, nx - 1)),
            dma((levels, nx - 1)),
            dma((nx - 1,)),
            dma((nx - 1,)),
            dma((2 * levels + 1,)),
        ],
        compiler_params=pltpu.CompilerParams(
            collective_id=0, has_side_effects=True, vmem_limit_bytes=48 << 20
        ),
    )(
        hidden, norm_gain.reshape(1, width), first_weight, second_weight, codes, codes.T,
        codebook, embed_avg, cluster_size,
    )


def solution(mesh):
    in_specs = (
        P(("code", "item"), None),
        P(),
        P("item", None),
        P("item", None),
        P(("code", "item"), None),
        P(None, "code", None),
        P(None, "code", None),
        P(None, "code"),
    )
    out_specs = (
        P(("code", "item"), None),
        P(None, "code"),
        P(None, "code", None),
        P(None, "code", None),
    )
    return jax.shard_map(body, mesh=mesh, in_specs=in_specs, out_specs=out_specs, check_vma=False)
```

time: 302 us -> 116 us (0.38)
  the two profiles are of different devices: /device:TPU:8 before, /device:TPU:24 now
where the time goes in v1:
time: 116 us
  Pallas kernels  106 us (91%)
  local copies, waits for them, and re-layouts  9.71 us (8%)
    pallas_call x1, Pallas kernels, body(): pl.pallas_call(functools.partial(kernel, cfg), out_shape=shapes, in_specs...  106 us
    unnamed x19, local copies, waits for them, and re-layouts  9.02 us

profile of v1, /device:TPU:24, one launch (start us, length us, event | category | flops | bytes accessed | tf_op | source)
XLA Modules:
  0.0 116.0 jit_solution(7247912817286560673)
XLA Ops:
  0.6 0.0 copy-start.5
  0.6 0.7 reshape.11.gain_ref
  1.3 0.0 copy-done.5
  1.3 0.0 copy-start.6
  1.3 0.1 copy.12.codes_ref
  1.5 0.6 copy-done.6
  2.0 0.0 copy-start
  2.0 1.1 copy-done
  3.2 0.0 copy-start.1
  3.2 1.1 copy-done.1
  4.3 0.0 copy-start.2
  4.3 1.0 copy-done.2
  5.3 0.0 copy-start.3
  5.3 1.0 copy-done.3
  6.4 0.0 copy-start.4
  6.4 0.9 copy-done.4
  7.3 105.6 %shard_map.111 = (bf16[128,1024]{1,0:T(8,128)(2,1)S(1)}, f32[3,64]{1,0:T(4,128)S(1)}, f32[3,64,1024]{2,1,0:T(8,128)S(1)}, f32[3,64,1024]{2,1,0:T(8,128)S(1)}) custom-call(bf16[128,1024]{1,0:T(8,128)(2,1)S(1)} %copy-done.4, bf16[1,1024]{1,0:T(2,128)(2,1)S(1)} %reshape.11.gain_ref, bf16[256,1024]{1,0:T(8,128)(2,1)S(1)} %copy-done.2, ...), custom_call_target="tpu_custom_call" | custom-call | tf_op jit(solution)/shard_map/pallas_call | solution.py:417
  112.9 0.7 copy.17
  113.7 0.6 copy.18
  114.2 0.9 copy.19
  115.1 0.9 copy.20
Async XLA Ops:
  0.6 0.7 copy-start.5
  1.3 0.7 copy-start.6
  2.0 1.1 copy-start
  3.2 1.1 copy-start.1
  4.3 1.0 copy-start.2
  5.3 1.0 copy-start.3
  6.4 0.9 copy-start.4

commit v2 on v1

--- a/solution.py
+++ b/solution.py
@@ -27,7 +27,7 @@
 
 def kernel(
     cfg,
-    hidden_ref, gain_ref, w1_ref, w2_ref, codes_ref, codes_t_ref, book_ref, embed_ref, size_ref,
+    hidden_ref, gain_ref, w1_ref, w2_ref, codes_ref, book_ref, embed_ref, size_ref,
     resid_out, cluster_out, avg_out, new_out,
     hid, book, embed, w1, w2, outv, avgv, newv,
     flat8, book8, r8, tot8, onehot, idxexp,
@@ -48,31 +48,41 @@
     xsum = (xsum0, xsum1, xsum2)
     me = lax.axis_index("code")
     xi = lax.axis_index("item")
-    core = me % CORES
-    z = (me // CORES) % nz
-    y = me // (CORES * nz)
+    core = lax.rem(me, CORES)
+    z = lax.rem(lax.div(me, CORES), nz)
+    y = lax.div(me, CORES * nz)
     yc = y * CORES + core
     sibling = me + 1 - 2 * core
+    cores = (core, 1 - core)
+    columns = [lax.rem(z + a, nz) for a in range(nz)]
 
     def code_id(ty, tz, tc):
         return (ty * nz + tz) * CORES + tc
 
-    def zmate(k):
-        tz = (z + k) % nz
-        return tz, code_id(y, tz, core)
-
-    def ymate(k):
-        tc = (core + k) % CORES
-        ty = (y + k // CORES) % ny
-        return ty, tc, code_id(ty, z, tc)
-
-    def partner(k):
-        d = k // CORES
-        dz = d % nz
-        tc = (core + k) % CORES
-        tz = (z + dz) % nz
-        ty = (y + dz + d // nz) % ny
-        return code_id(ty, tz, tc), (ty * CORES + tc), tz
+    zmates = [(columns[a], code_id(y, columns[a], core)) for a in range(1, nz)]
+    ymates = [
+        (lax.rem(y + a, ny) * CORES + cores[c], code_id(lax.rem(y + a, ny), z, cores[c]))
+        for a in range(ny)
+        for c in range(CORES)
+        if (a, c) != (0, 0)
+    ]
+
+    def sweep(build, send, turn):
+        def group(b, first=False):
+            partners = []
+            for a in range(nz):
+                tz = columns[turn[0] * a % nz]
+                ty = lax.rem(y + 2 * ny + turn[1] * (a + b), ny)
+                for c in range(CORES):
+                    if not (first and a == 0 and c == 0):
+                        partners.append((code_id(ty, tz, cores[c]), ty * CORES + cores[c], tz))
+            for one in partners:
+                build(*one)
+            for one in partners:
+                send(one[0])
+
+        group(0, first=True)
+        loop(1, ny, group)
 
     def loop(low, high, step, unroll=1):
         def go(k, _):
@@ -99,10 +109,10 @@
     def greet(device):
         pl.semaphore_signal(barrier, inc=1, device_id=device, device_id_type=MESH)
 
-    loop(1, nz, lambda k: greet({"code": zmate(k)[1]}))
-    loop(1, nyc, lambda k: greet({"code": ymate(k)[2]}))
+    for _, device in zmates + ymates:
+        greet({"code": device})
     for d in range(1, nx):
-        greet({"item": (xi + d) % nx})
+        greet({"item": lax.rem(xi + d, nx)})
 
     lane = iota((rows, LANES), 1)
     down, across = iota((rows, rows), 0), iota((rows, rows), 1)
@@ -112,8 +122,9 @@
     items[...] = jnp.zeros(items.shape, I32)
     slots[...] = jnp.zeros(slots.shape, I32)
     for level in range(levels):
-        code_col, code_row = codes_ref[:, level : level + 1], codes_t_ref[level : level + 1, :]
-        owner_col, owner_row = code_col // code_dev, code_row // code_dev
+        code_row = codes_ref[level : level + 1, :]
+        owner_row = code_row // code_dev
+        owner_col = jnp.sum(jnp.where(down == across, owner_row, 0), axis=1, keepdims=True)
         same = owner_col == owner_row
         rank_row = jnp.sum(jnp.where(same & (down < across), 1, 0), axis=0, keepdims=True)
         rank_col = jnp.sum(jnp.where(same & (across < down), 1, 0), axis=1, keepdims=True)
@@ -135,58 +146,51 @@
     for one in to_smem:
         one.start()
 
-    loads[0].wait()
-    values = hid[...].astype(F32)
-    power = jnp.mean(values * values, axis=-1, keepdims=True)
-    normed = (values * lax.rsqrt(power + norm_eps) * gain_ref[...].astype(F32)).astype(BF16)
-    hid[...] = normed
+    pl.semaphore_wait(barrier, nz - 1 + nyc - 1 + nx - 1)
+
+    def ring_rows(tz):
+        return pl.ds(pl.multiple_of(tz * nyc, nyc), nyc)
+
+    for tz, device in zmates:
+        pltpu.make_async_remote_copy(
+            src_ref=table.at[ring_rows(tz)], dst_ref=zgot.at[z], send_sem=zsend, recv_sem=zrecv,
+            device_id={"code": device}, device_id_type=MESH,
+        ).start()
+
+    zgot[z] = table[ring_rows(z), :]
+
+    half = w1.shape[1] // CORES
+    weights = (w1, w2)
+
+    def part(w, source, which):
+        return w.at[source, pl.ds(pl.multiple_of(which * half, half), half)]
+
+    def weight_copy(i, d):
+        return pltpu.make_async_remote_copy(
+            src_ref=part(weights[i], xi, core), dst_ref=part(weights[i], xi, core),
+            send_sem=wsend.at[i, d - 1], recv_sem=wrecv.at[i, d - 1],
+            device_id={"item": lax.rem(xi + d, nx)}, device_id_type=MESH,
+        )
+
+    def pass_on(i, d):
+        source = lax.rem(xi + nx - d, nx)
+        return pltpu.make_async_remote_copy(
+            src_ref=part(weights[i], source, core), dst_ref=part(weights[i], source, core),
+            send_sem=fsend.at[i, d - 1], recv_sem=frecv.at[i, d - 1],
+            device_id={"code": sibling}, device_id_type=MESH,
+        )
+
+    for i in range(2):
+        loads[2 + i].wait()
+        for d in range(1, nx):
+            weight_copy(i, d).start()
+
     loads[1].wait()
     for level in range(levels):
         for c in range(CHUNKS):
             flat8[pl.ds(c, code_dev, stride=CHUNKS), :] = book[level, :, c * LANES : (c + 1) * LANES]
         book8[level] = flat8[: code_dev * CHUNKS, :].reshape(code_dev, CHUNKS, LANES)
-    for one in loads[2:]:
-        one.wait()
-
-    pl.semaphore_wait(barrier, nz - 1 + nyc - 1 + nx - 1)
-
-    def ring_rows(tz):
-        return pl.ds(pl.multiple_of(tz * nyc, nyc), nyc)
-
-    def send_table(k):
-        tz, device = zmate(k)
-        pltpu.make_async_remote_copy(
-            src_ref=table.at[ring_rows(tz)], dst_ref=zgot.at[z], send_sem=zsend, recv_sem=zrecv,
-            device_id={"code": device}, device_id_type=MESH,
-        ).start()
-
-    loop(1, nz, send_table)
-    zgot[z] = table[ring_rows(z), :]
-
-    half = w1.shape[1] // CORES
-    weights = (w1, w2)
-
-    def part(w, source, which):
-        return w.at[source, pl.ds(pl.multiple_of(which * half, half), half)]
-
-    def weight_copy(i, d):
-        return pltpu.make_async_remote_copy(
-            src_ref=part(weights[i], xi, core), dst_ref=part(weights[i], xi, core),
-            send_sem=wsend.at[i, d - 1], recv_sem=wrecv.at[i, d - 1],
-            device_id={"item": (xi + d) % nx}, device_id_type=MESH,
-        )
-
-    def pass_on(i, d):
-        source = (xi + nx - d) % nx
-        return pltpu.make_async_remote_copy(
-            src_ref=part(weights[i], source, core), dst_ref=part(weights[i], source, core),
-            send_sem=fsend.at[i, d - 1], recv_sem=frecv.at[i, d - 1],
-            device_id={"code": sibling}, device_id_type=MESH,
-        )
-
-    for i in range(2):
-        for d in range(1, nx):
-            weight_copy(i, d).start()
+
 
     wait_bytes(zgot.at[pl.ds(0, nz - 1)], zrecv)
     gathered = zgot[0]
@@ -195,21 +199,19 @@
     ysrc[:nyc, :] = gathered
 
     def tile_of(at):
-        return pl.ds(pl.multiple_of(at // 8 * 8, 8), 8)
-
-    def send_requests(k):
-        ty, tc, device = ymate(k)
+        return pl.ds(pl.multiple_of(lax.div(at, 8) * 8, 8), 8)
+
+    for tyc, device in ymates:
         pltpu.make_async_remote_copy(
-            src_ref=ysrc.at[tile_of(ty * CORES + tc)], dst_ref=ygot.at[yc], send_sem=ysend, recv_sem=yrecv,
+            src_ref=ysrc.at[tile_of(tyc)], dst_ref=ygot.at[yc], send_sem=ysend, recv_sem=yrecv,
             device_id={"code": device}, device_id_type=MESH,
         ).start()
 
-    loop(1, nyc, send_requests)
     ygot[yc] = ysrc[tile_of(yc), :]
     for one in to_smem:
         one.wait()
     wait_bytes(ygot.at[pl.ds(0, nyc - 1)], yrecv)
-    mine = iota((nyc, 8, LANES), 1) == yc % 8
+    mine = iota((nyc, 8, LANES), 1) == lax.rem(yc, 8)
     want[...] = jnp.sum(jnp.where(mine, ygot[...], 0), axis=1) - 1
     picked[...] = jnp.maximum(want[...], 0)
     ask = pltpu.make_async_copy(picked, want_s, ssem.at[2])
@@ -231,47 +233,50 @@
     count_copies = [
         pltpu.make_async_remote_copy(
             src_ref=xcount.at[xi], dst_ref=xcount.at[xi], send_sem=css.at[d - 1], recv_sem=crs.at[d - 1],
-            device_id={"item": (xi + d) % nx}, device_id_type=MESH,
+            device_id={"item": lax.rem(xi + d, nx)}, device_id_type=MESH,
         )
         for d in range(1, nx)
     ]
     ask.wait()
 
+    reply_turns = ((1, 1), (-1, -1), (-1, -1))
+    row_turns = ((1, -1), (-1, 1), (1, 1))
+
     def reply(level):
-        def block(rs):
-            rows_of = [book8[level, want_s[rs[0], rs[1] * 8 + 2 * level + k]] for k in range(2)]
+        def block(tyc, tz):
+            rows_of = [book8[level, want_s[tyc, tz * 8 + (2 * level + k)]] for k in range(2)]
             return jnp.concatenate(rows_of, axis=0).astype(BF16)
 
-        qrecv[level][me] = block((yc, z))
-
-        def one(k):
-            device, tyc, tz = partner(k)
-            qsend[level][device] = block((tyc, tz))
+        def build(device, tyc, tz):
+            qsend[level][device] = block(tyc, tz)
+
+        def send(device):
             pltpu.make_async_remote_copy(
                 src_ref=qsend[level].at[device], dst_ref=qrecv[level].at[me],
                 send_sem=qss.at[level], recv_sem=qrs.at[level],
                 device_id={"code": device}, device_id_type=MESH,
             ).start()
 
-        loop(1, owners, one)
+        qrecv[level][me] = block(yc, z)
+        sweep(build, send, reply_turns[level])
 
     def send_rows(level):
         def block(owner):
             rows_of = [r8[items_s[2 * level + k, owner]] for k in range(2)]
             return jnp.concatenate(rows_of, axis=0).astype(BF16)
 
-        rrecv[level][yc * nz + z] = block(me)
-
-        def one(k):
-            device, _, _ = partner(k)
+        def build(device, tyc, tz):
             rsend[level][device] = block(device)
+
+        def send(device):
             pltpu.make_async_remote_copy(
                 src_ref=rsend[level].at[device], dst_ref=rrecv[level].at[yc * nz + z],
                 send_sem=rss.at[level], recv_sem=rrs.at[level],
                 device_id={"code": device}, device_id_type=MESH,
             ).start()
 
-        loop(1, owners, one)
+        rrecv[level][yc * nz + z] = block(me)
+        sweep(build, send, row_turns[level])
 
     def subtract(level):
         wait_bytes(qrecv[level].at[pl.ds(0, owners - 1)], qrs.at[level])
@@ -281,7 +286,7 @@
             pair = qrecv[level][slots_s[level, i]].astype(F32)
             r8[i] = r8[i] - (pair[:CHUNKS] * (1.0 - second) + pair[CHUNKS:] * second)
 
-        loop(0, rows, one, unroll=4)
+        loop(0, rows, one, unroll=8)
 
     reply(0)
     for one in count_copies:
@@ -293,6 +298,15 @@
     for d in range(1, nx):
         weight_copy(1, d).wait_recv()
         pass_on(1, d).start()
+
+    loads[0].wait()
+    values = hid[...].astype(F32)
+    power = jnp.mean(values * values, axis=-1, keepdims=True)
+    scaled = values * lax.rsqrt(power + norm_eps)
+    gain = gain_ref[...].astype(F32)
+    for c in range(CHUNKS):
+        span = slice(c * LANES, (c + 1) * LANES)
+        hid[:, span] = (scaled[:, span] * gain[c : c + 1, :]).astype(BF16)
 
     depth = w1.shape[1] * nx
     for d in range(1, nx):
@@ -310,7 +324,7 @@
         return pltpu.make_async_remote_copy(
             src_ref=xsum[level].at[xi], dst_ref=xsum[level].at[xi],
             send_sem=xss.at[level, d - 1], recv_sem=xrs.at[level, d - 1],
-            device_id={"item": (xi + d) % nx}, device_id_type=MESH,
+            device_id={"item": lax.rem(xi + d, nx)}, device_id_type=MESH,
         )
 
     def add_up(level):
@@ -354,6 +368,7 @@
         for one in out_copies(level):
             one.start()
 
+    loads[4].wait()
     send_rows(0)
     subtract(0)
     send_rows(1)
@@ -417,7 +432,7 @@
     return pl.pallas_call(
         functools.partial(kernel, cfg),
         out_shape=shapes,
-        in_specs=[anywhere, inside, anywhere, anywhere, inside, inside, anywhere, anywhere, inside],
+        in_specs=[anywhere, inside, anywhere, anywhere, inside, anywhere, anywhere, inside],
         out_specs=(anywhere, inside, anywhere, anywhere),
         scratch_shapes=[
             vmem((rows, width), BF16),
@@ -469,10 +484,10 @@
             dma((2 * levels + 1,)),
         ],
         compiler_params=pltpu.CompilerParams(
-            collective_id=0, has_side_effects=True, vmem_limit_bytes=48 << 20
+            collective_id=0, has_side_effects=True, vmem_limit_bytes=64 << 20
         ),
     )(
-        hidden, norm_gain.reshape(1, width), first_weight, second_weight, codes, codes.T,
+        hidden, norm_gain.reshape(CHUNKS, LANES), first_weight, second_weight, codes.T,
         codebook, embed_avg, cluster_size,
     )
 

time: 116 us -> 111 us (0.957)
  the two profiles are of different devices: /device:TPU:24 before, /device:TPU:193 now
where the time goes in v2:
time: 111 us
  Pallas kernels  105 us (95%)
  local copies, waits for them, and re-layouts  5.3 us (5%)
    pallas_call x1, Pallas kernels, body(): pl.pallas_call(functools.partial(kernel, cfg), out_shape=shapes, in_specs...  105 us
    unnamed x8, local copies, waits for them, and re-layouts  5.3 us

profile of v2, /device:TPU:193, one launch (start us, length us, event | category | flops | bytes accessed | tf_op | source)
XLA Modules:
  0.0 111.1 jit_solution(7895780801438384161)
XLA Ops:
  0.6 105.2 %shard_map.111 = (bf16[128,1024]{1,0:T(8,128)(2,1)}, f32[3,64]{1,0:T(4,128)}, f32[3,64,1024]{2,1,0:T(8,128)}, f32[3,64,1024]{2,1,0:T(8,128)}) custom-call(bf16[128,1024]{1,0:T(8,128)(2,1)} %hidden_ref.1, bf16[8,128]{1,0:T(8,128)(2,1)} %bitcast.2, bf16[256,1024]{1,0:T(8,128)(2,1)} %w1_ref.1, bf16[256,1024]{1,0:T(8,128)(2,1)} %w2_ref.1, s32[3,128]{1,0:T(4,128)} %bitcast.3, ...), custom_call_target="tpu_custom_call" | custom-call | tf_op jit(solution)/shard_map/pallas_call | solution.py:432
  105.8 0.0 copy-start.1
  105.8 1.7 %copy.16 = bf16[128,1024]{1,0:T(8,128)(2,1)} copy(bf16[128,1024]{1,0:T(8,128)(2,1)} %get-tuple-element.8) | data formatting | bytes 524288
  107.5 0.0 copy-done.1
  107.5 0.6 copy.17
  108.1 0.0 copy-start
  108.1 2.2 %copy.18 = f32[3,64,1024]{2,1,0:T(8,128)} copy(f32[3,64,1024]{2,1,0:T(8,128)} %get-tuple-element.10) | data formatting | bytes 1572864
  110.2 0.0 copy-done
  110.2 0.9 copy.19
Async XLA Ops:
  105.8 1.7 %copy-start.1 = (f32[3,64]{1,0:T(4,128)S(1)}, f32[3,64]{1,0:T(4,128)}, u32[]{:S(2)}) copy-start(f32[3,64]{1,0:T(4,128)} %get-tuple-element.9) | copy-start | bytes 2308
  108.1 2.2 %copy-start = (f32[3,64,1024]{2,1,0:T(8,128)S(1)}, f32[3,64,1024]{2,1,0:T(8,128)}, u32[]{:S(2)}) copy-start(f32[3,64,1024]{2,1,0:T(8,128)} %get-tuple-element.11) | copy-start | bytes 2359300

commit v3 on v2

--- a/solution.py
+++ b/solution.py
@@ -29,7 +29,7 @@
     cfg,
     hidden_ref, gain_ref, w1_ref, w2_ref, codes_ref, book_ref, embed_ref, size_ref,
     resid_out, cluster_out, avg_out, new_out,
-    hid, book, embed, w1, w2, outv, avgv, newv,
+    hid, book, embed, w1, w2, outv, avgv, newv, cluster,
     flat8, book8, r8, tot8, onehot, idxexp,
     table, items, slots, zgot, ysrc, ygot, want, picked, xcount,
     items_s, slots_s, want_s,
@@ -71,8 +71,12 @@
         def group(b, first=False):
             partners = []
             for a in range(nz):
-                tz = columns[turn[0] * a % nz]
-                ty = lax.rem(y + 2 * ny + turn[1] * (a + b), ny)
+                if turn[2]:
+                    tz = lax.rem(z + 2 * nz + turn[0] * (a + b), nz)
+                    ty = lax.rem(y + ny + turn[1] * a, ny)
+                else:
+                    tz = columns[turn[0] * a % nz]
+                    ty = lax.rem(y + 2 * ny + turn[1] * (a + b), ny)
                 for c in range(CORES):
                     if not (first and a == 0 and c == 0):
                         partners.append((code_id(ty, tz, cores[c]), ty * CORES + cores[c], tz))
@@ -239,8 +243,8 @@
     ]
     ask.wait()
 
-    reply_turns = ((1, 1), (-1, -1), (-1, -1))
-    row_turns = ((1, -1), (-1, 1), (1, 1))
+    reply_turns = ((1, 1, 0), (-1, -1, 1), (1, -1, 1))
+    row_turns = ((1, -1, 0), (-1, 1, 1), (-1, -1, 0))
 
     def reply(level):
         def block(tyc, tz):
@@ -356,7 +360,7 @@
         for x in range(1, nx):
             total = total + xsum[level][x].astype(F32)
         tot8[...] = total
-        row = cluster_out[level : level + 1, :]
+        row = cluster[level : level + 1, :]
         same = iota((code_dev, code_dev), 0) == iota((code_dev, code_dev), 1)
         column = jnp.sum(jnp.where(same, row, 0.0), axis=1, keepdims=True)
         for c in range(CHUNKS):
@@ -379,7 +383,9 @@
     counts = xcount[0]
     for x in range(1, nx):
         counts = counts + xcount[x]
-    cluster_out[...] = ema_decay * size_ref[...] + (1.0 - ema_decay) * counts[:levels, :code_dev]
+    cluster[...] = ema_decay * size_ref[...] + (1.0 - ema_decay) * counts[:levels, :code_dev]
+    cluster_copy = pltpu.make_async_copy(cluster, cluster_out, lsem.at[0])
+    cluster_copy.start()
     add_up(0)
     reply(2)
     add_up(1)
@@ -409,6 +415,23 @@
         for one in out_copies(level):
             one.wait()
     last.wait()
+    cluster_copy.wait()
+
+
+def settle(levels, *refs):
+    sources, targets, held, came, went = refs[:4], refs[4:8], refs[8:12], refs[12], refs[13]
+    views = [(sources[i], held[i], targets[i]) for i in (0, 1)]
+    for level in range(levels):
+        views += [(sources[i].at[level], held[i].at[level], targets[i].at[level]) for i in (2, 3)]
+    loads = [pltpu.make_async_copy(a, b, came.at[i]) for i, (a, b, _) in enumerate(views)]
+    stores = [pltpu.make_async_copy(b, c, went.at[i]) for i, (_, b, c) in enumerate(views)]
+    for one in loads:
+        one.start()
+    for load, store in zip(loads, stores):
+        load.wait()
+        store.start()
+    for one in stores:
+        one.wait()
 
 
 def body(hidden, norm_gain, first_weight, second_weight, codes, codebook, embed_avg, cluster_size):
@@ -429,11 +452,11 @@
         jax.ShapeDtypeStruct((levels, code_dev, width), F32),
         jax.ShapeDtypeStruct((levels, code_dev, width), F32),
     )
-    return pl.pallas_call(
+    results = pl.pallas_call(
         functools.partial(kernel, cfg),
         out_shape=shapes,
         in_specs=[anywhere, inside, anywhere, anywhere, inside, anywhere, anywhere, inside],
-        out_specs=(anywhere, inside, anywhere, anywhere),
+        out_specs=(anywhere, anywhere, anywhere, anywhere),
         scratch_shapes=[
             vmem((rows, width), BF16),
             vmem((levels, code_dev, width), F32),
@@ -443,6 +466,7 @@
             vmem((rows, width), BF16),
             vmem((levels, code_dev, width), F32),
             vmem((levels, code_dev, width), F32),
+            vmem((levels, code_dev), F32),
             vmem((max(rows, code_dev) * CHUNKS, LANES), F32),
             vmem((levels, code_dev, CHUNKS, LANES), F32),
             vmem((rows, CHUNKS, LANES), F32),
@@ -490,6 +514,14 @@
         hidden, norm_gain.reshape(CHUNKS, LANES), first_weight, second_weight, codes.T,
         codebook, embed_avg, cluster_size,
     )
+    return pl.pallas_call(
+        functools.partial(settle, levels),
+        out_shape=shapes,
+        in_specs=[anywhere] * 4,
+        out_specs=(anywhere,) * 4,
+        scratch_shapes=[vmem(x.shape, x.dtype) for x in shapes] + [dma((2 + 2 * levels,))] * 2,
+        compiler_params=pltpu.CompilerParams(vmem_limit_bytes=64 << 20),
+    )(*results)
 
 
 def solution(mesh):

time: 111 us -> 107 us (0.964)
  the two profiles are of different devices: /device:TPU:193 before, /device:TPU:48 now
where the time goes in v3:
time: 107 us; the launch traced here: 106 us
  Pallas kernels  106 us (99%)
    pallas_call x1, Pallas kernels, body(): pl.pallas_call(functools.partial(kernel, cfg), out_shape=shapes, in_specs...  103 us
    pallas_call x1, Pallas kernels, body(): pl.pallas_call(functools.partial(settle, levels), out_shape=shapes, in_sp...  2.31 us

profile of v3, /device:TPU:48, one launch (start us, length us, event | category | flops | bytes accessed | tf_op | source)
XLA Modules:
  0.0 106.4 jit_solution(12098834564957864646)
XLA Ops:
  0.6 103.5 %shard_map.111 = (bf16[128,1024]{1,0:T(8,128)(2,1)}, f32[3,64]{1,0:T(4,128)}, f32[3,64,1024]{2,1,0:T(8,128)}, f32[3,64,1024]{2,1,0:T(8,128)}) custom-call(bf16[128,1024]{1,0:T(8,128)(2,1)} %hidden_ref.1, bf16[8,128]{1,0:T(8,128)(2,1)} %bitcast.2, bf16[256,1024]{1,0:T(8,128)(2,1)} %w1_ref.1, bf16[256,1024]{1,0:T(8,128)(2,1)} %w2_ref.1, s32[3,128]{1,0:T(4,128)} %bitcast.3, ...), custom_call_target="tpu_custom_call" | custom-call | tf_op jit(solution)/shard_map/pallas_call | solution.py:455
  104.1 2.3 %shard_map.112 = (bf16[128,1024]{1,0:T(8,128)(2,1)}, f32[3,64]{1,0:T(4,128)}, f32[3,64,1024]{2,1,0:T(8,128)}, f32[3,64,1024]{2,1,0:T(8,128)}) custom-call(bf16[128,1024]{1,0:T(8,128)(2,1)} %get-tuple-element.8.refs_0_, f32[3,64]{1,0:T(4,128)} %get-tuple-element.9.refs_1_, f32[3,64,1024]{2,1,0:T(8,128)} %get-tuple-element.10.refs_2_, ...), custom_call_target="tpu_custom_call" | custom-call | tf_op jit(solution)/shard_map/pallas_call | solution.py:517

commit v4 on v3

--- a/solution.py
+++ b/solution.py
@@ -85,8 +85,8 @@
             for one in partners:
                 send(one[0])
 
+        loop(1, ny, group)
         group(0, first=True)
-        loop(1, ny, group)
 
     def loop(low, high, step, unroll=1):
         def go(k, _):

time: 107 us -> 104 us (0.972)
  the two profiles are of different devices: /device:TPU:48 before, /device:TPU:193 now
where the time goes in v4:
time: 104 us
  Pallas kernels  103 us (99%)
    pallas_call x1, Pallas kernels, body(): pl.pallas_call(functools.partial(kernel, cfg), out_shape=shapes, in_specs...  101 us
    pallas_call x1, Pallas kernels, body(): pl.pallas_call(functools.partial(settle, levels), out_shape=shapes, in_sp...  2.31 us

profile of v4, /device:TPU:193, one launch (start us, length us, event | category | flops | bytes accessed | tf_op | source)
XLA Modules:
  0.0 103.7 jit_solution(6115509025008503363)
XLA Ops:
  0.6 100.7 %shard_map.111 = (bf16[128,1024]{1,0:T(8,128)(2,1)}, f32[3,64]{1,0:T(4,128)}, f32[3,64,1024]{2,1,0:T(8,128)}, f32[3,64,1024]{2,1,0:T(8,128)}) custom-call(bf16[128,1024]{1,0:T(8,128)(2,1)} %hidden_ref.1, bf16[8,128]{1,0:T(8,128)(2,1)} %bitcast.2, bf16[256,1024]{1,0:T(8,128)(2,1)} %w1_ref.1, bf16[256,1024]{1,0:T(8,128)(2,1)} %w2_ref.1, s32[3,128]{1,0:T(4,128)} %bitcast.3, ...), custom_call_target="tpu_custom_call" | custom-call | tf_op jit(solution)/shard_map/pallas_call | solution.py:455
  101.4 2.3 %shard_map.112 = (bf16[128,1024]{1,0:T(8,128)(2,1)}, f32[3,64]{1,0:T(4,128)}, f32[3,64,1024]{2,1,0:T(8,128)}, f32[3,64,1024]{2,1,0:T(8,128)}) custom-call(bf16[128,1024]{1,0:T(8,128)(2,1)} %get-tuple-element.8.refs_0_, f32[3,64]{1,0:T(4,128)} %get-tuple-element.9.refs_1_, f32[3,64,1024]{2,1,0:T(8,128)} %get-tuple-element.10.refs_2_, ...), custom_call_target="tpu_custom_call" | custom-call | tf_op jit(solution)/shard_map/pallas_call | solution.py:517
